TPU v7x, 32 devices: a whole 2x2x4 slice. The times are simulated.
32 devices in a mesh: section: 2 (over x), tensor: 4 (over y, core), dp: 4 (over z).
Axes of the slice: x: 2, y: 2, z: 4, core: 2. Of those that a mesh axis runs over, the one named last changes fastest.
Arguments:
- patches: bfloat16 [32, 102, 768], P('dp'), may hold values from -6 to 6
- cotangent: bfloat16 [32, 512, 512], P('dp'), may hold values from -6 to 6
- widths: int32 [32], P('dp'), may hold values from 4 to 8, as said below
- visible: int32 [32, 102], P('dp'), may hold values from 0 to 511, as said below
- window_shift: int32 [32, 2], P('dp'), may hold values from 0 to 3
- batch_order: int32 [4, 8], P('dp'), may hold values from 0 to 7, each once within a row
- encoder_qkv: bfloat16 [768, 3, 768], P(None, None, 'tensor'), may hold values from -0.21875 to 0.21875
- encoder_qvbias: bfloat16 [2, 768], P(None, 'tensor'), may hold values from -1.796875 to 1.796875
- encoder_proj: bfloat16 [768, 768], P('tensor'), may hold values from -0.625 to 0.625
- encoder_up: bfloat16 [768, 3072], P(None, 'tensor'), may hold values from -0.21875 to 0.21875
- encoder_upbias: bfloat16 [3072], P('tensor'), may hold values from -1.796875 to 1.796875
- encoder_down: bfloat16 [3072, 768], P('tensor'), may hold values from -0.109375 to 0.109375
- encoder_gains: bfloat16 [2, 768], replicated, may hold values from 0.099609375 to 1.8984375
- encoder_offsets: bfloat16 [4, 768], replicated, may hold values from -1.796875 to 1.796875
- decoder_qkv: bfloat16 [512, 3, 512], P(None, None, 'tensor'), may hold values from -0.25 to 0.25
- decoder_qvbias: bfloat16 [2, 512], P(None, 'tensor'), may hold values from -1.796875 to 1.796875
- decoder_proj: bfloat16 [512, 512], P('tensor'), may hold values from -0.5 to 0.5
- decoder_up: bfloat16 [512, 2048], P(None, 'tensor'), may hold values from -0.25 to 0.25
- decoder_upbias: bfloat16 [2048], P('tensor'), may hold values from -1.796875 to 1.796875
- decoder_down: bfloat16 [2048, 512], P('tensor'), may hold values from -0.125 to 0.125
- decoder_gains: bfloat16 [2, 512], replicated, may hold values from 0.099609375 to 1.8984375
- decoder_offsets: bfloat16 [4, 512], replicated, may hold values from -1.796875 to 1.796875
- embed_weight: bfloat16 [768, 512], replicated, may hold values from -0.21875 to 0.21875
- embed_vectors: bfloat16 [2, 512], replicated, may hold values from -3 to 3
Outputs:
- decoded: bfloat16 [32, 512, 512], P('dp', None, ('section', 'tensor'))
- patches_grad: bfloat16 [32, 102, 768], P('dp', None, ('section', 'tensor'))
- encoder_qkv_grad: float32 [768, 3, 768], P(None, None, 'tensor')
- encoder_qvbias_grad: float32 [2, 768], P(None, 'tensor')
- encoder_proj_grad: float32 [768, 768], P('tensor')
- encoder_up_grad: float32 [768, 3072], P(None, 'tensor')
- encoder_upbias_grad: float32 [3072], P('tensor')
- encoder_down_grad: float32 [3072, 768], P('tensor')
- encoder_gains_grad: float32 [2, 768], replicated
- encoder_offsets_grad: float32 [4, 768], replicated
- decoder_qkv_grad: float32 [512, 3, 512], P(None, None, 'tensor')
- decoder_qvbias_grad: float32 [2, 512], P(None, 'tensor')
- decoder_proj_grad: float32 [512, 512], P('tensor')
- decoder_up_grad: float32 [512, 2048], P(None, 'tensor')
- decoder_upbias_grad: float32 [2048], P('tensor')
- decoder_down_grad: float32 [2048, 512], P('tensor')
- decoder_gains_grad: float32 [2, 512], replicated
- decoder_offsets_grad: float32 [4, 512], replicated
- embed_weight_grad: float32 [768, 512], replicated
- embed_vectors_grad: float32 [2, 512], replicated
Inputs may be any that keep to these rules, and one draw needn't show every extreme that they name: `widths`: each clip's grid is 64 rows by its width, which is 8 or 4. `visible`: within a clip the 102 entries are distinct. For a clip of width w the first 102 * w // 8 entries lie below 64 * w and the others at or above it. `batch_order`: each row is a permutation of the 8 clips of one index of dp.
All inputs are finite; a program needn't handle non-finite values.
Results may differ from a plain program's by a relative error of at most 0.025.
Values may be sent and summed in bfloat16 or wider, within the bound.
A program may use at most 256 MiB of HBM per device.

v0:
```python
import math

import jax
import jax.numpy as jnp
import numpy as np
from jax import lax
from jax.experimental import pallas as pl
from jax.experimental.pallas import tpu as pltpu
from jax.sharding import PartitionSpec as P

D = 768
HEADS = 12
DD = 512
DHEADS = 16
GRID_ROWS = 64
WIDE = 8
WIN = 4
VIS = 102
CM = 4
GRID = 512
LANES = 4
PAD = 128
EPS = 1e-06
NEG = -10000.0
F32 = jnp.float32
BF16 = jnp.bfloat16
VMEM_LIMIT = 60 * 1024 * 1024

VM = pl.BlockSpec(memory_space=pltpu.VMEM)
SM = pl.BlockSpec(memory_space=pltpu.SMEM)
ANY = pl.BlockSpec(memory_space=pl.ANY)


def nn(a, b):
    return lax.dot_general(a, b, (((1,), (0,)), ((), ())), preferred_element_type=F32)


def nt(a, b):
    return lax.dot_general(a, b, (((1,), (1,)), ((), ())), preferred_element_type=F32)


def tn(a, b):
    return lax.dot_general(a, b, (((0,), (0,)), ((), ())), preferred_element_type=F32)


def loop(count, body, unroll=1):
    def step(i, carry):
        body(i)
        return carry

    lax.fori_loop(0, count, step, 0, unroll=unroll)


def span(i, size):
    return pl.ds(pl.multiple_of(i * size, size), size)


def normal(x):
    center = x - jnp.mean(x, -1, keepdims=True)
    scale = lax.rsqrt(jnp.mean(center * center, -1, keepdims=True) + EPS)
    return center * scale, scale


def normal_back(dy, hat, scale, gain):
    d = dy * gain
    return scale * (
        d - jnp.mean(d, -1, keepdims=True) - hat * jnp.mean(d * hat, -1, keepdims=True)
    )


def gelu_both(h):
    phi = 0.5 * lax.erf(h * math.sqrt(0.5)) + 0.5
    bell = jnp.exp2(h * h * (-0.5 * math.log2(math.e)))
    return h * phi, phi + h * bell * (1.0 / math.sqrt(2.0 * math.pi))


def colsum(x):
    return jnp.sum(x, 0, keepdims=True)


def head_marks(width, size, dtype):
    lane = lax.broadcasted_iota(jnp.int32, (1, width), 1)
    return [((lane >= h * size) & (lane < (h + 1) * size)).astype(dtype) for h in range(width // size)]


def stacked(x, marks):
    return jnp.concatenate([x * m for m in marks], 0)


LOG2E = math.log2(math.e)


def attend(q, k, v, marks, ones, masked, scale):
    keys = k.shape[0]
    s = nt(q, stacked(k, marks))
    parts = []
    for h in range(len(marks)):
        x = masked(s[:, h * keys : (h + 1) * keys] * (scale * LOG2E))
        parts.append(jnp.exp2(x - jnp.max(x, -1, keepdims=True)).astype(BF16))
    e = jnp.concatenate(parts, 1)
    width = q.shape[1]
    if width % 128:
        top, total = nn(e, stacked(v, marks)), nn(e, ones)
    else:
        both = nn(e, jnp.concatenate([stacked(v, marks), ones], 1))
        top, total = both[:, :width], both[:, width:]
    inverse = 1.0 / total
    return e, (top * inverse).astype(BF16), inverse


def attend_back(q, k, v, e, o, inverse, d_out, marks, marks32, rows32, ones, scale):
    keys = k.shape[0]
    width = q.shape[1]
    d_one = d_out.astype(F32) * inverse
    d_two = (d_one * o.astype(F32)).astype(BF16)
    d_one = d_one.astype(BF16)
    if width % 128:
        d_s = nt(d_one, stacked(v, marks)) - nt(d_two, ones)
    else:
        d_s = nt(
            jnp.concatenate([d_one, d_two], 1), jnp.concatenate([stacked(v, marks), -ones], 1)
        )
    dr = (e.astype(F32) * d_s * scale).astype(BF16)
    d_q = nn(dr, stacked(k, marks)).astype(BF16)
    if width % 128:
        d_k_all, d_v_all = tn(dr, q), tn(e, d_one)
        d_k = d_v = 0.0
        for h in range(len(marks)):
            cut = slice(h * keys, (h + 1) * keys)
            d_k += d_k_all[cut] * marks32[h]
            d_v += d_v_all[cut] * marks32[h]
        return d_q, d_k.astype(BF16), d_v.astype(BF16)
    d_k_all = nn(jnp.transpose(q.astype(F32)).astype(BF16), dr)
    d_v_all = nn(jnp.transpose(d_one.astype(F32)).astype(BF16), e)
    d_k = d_v = 0.0
    for h in range(len(marks)):
        cut = slice(h * keys, (h + 1) * keys)
        d_k += d_k_all[:, cut] * rows32[h]
        d_v += d_v_all[:, cut] * rows32[h]
    return d_q, jnp.transpose(d_k).astype(BF16), jnp.transpose(d_v).astype(BF16)


def ones_per_head(keys, marks):
    return jnp.concatenate([jnp.broadcast_to(m, (keys, m.shape[1])) for m in marks], 0)


ENC_SIZE = D // HEADS
ENC_SCALE = ENC_SIZE ** -0.5
DEC_SIZE = DD // DHEADS
DEC_SCALE = DEC_SIZE ** -0.5


CH = 64
DEC_ROWS = 576
ENC_A = 768
ENC_B = 384
DEC_K = DEC_ROWS // CH
B_K = (DEC_ROWS + ENC_A + ENC_B) // CH
ALL_K = B_K + 1
A_TOP = DEC_ROWS
B_TOP = DEC_ROWS + ENC_A
S_TOP = B_TOP + ENC_B
EARLY = 4
EARLY_ROWS = EARLY * CH
LAG = 2
MIXED = EARLY + 2 * (DEC_K - EARLY)
WAIT = 2
LATE = 16
HALVED = ALL_K - 4


def tile_of(number):
    place = number // 3
    return place % 2, place // 2 * CH, number % 3 * 256


MESH = pl.DeviceIdType.MESH


def far(src, dst, send, recv, peer):
    return pltpu.make_async_remote_copy(
        src_ref=src, dst_ref=dst, send_sem=send, recv_sem=recv, device_id=peer, device_id_type=MESH
    )


def forward_and_decoder(
    wid, shifts, order, vis, pat, gains, offs, b_qv, b_up, b_dqv, b_dup,
    h_qkv, h_proj, h_up, h_down, h_dqkv, h_dproj, h_dup, h_ddown,
    cot_hbm, ew, evec, table, dgains, doffs,
    o_x, o_x1, o_a, o_u, o_y, o_gp, o_qkv, o_p, o_o, o_w, o_wproj, o_wup, o_wdown, o_dec,
    d_enc, d_qvb, d_upb, d_small, dec_out,
    w_qkv, w_proj, w_up, w_down, bias, biases, qkv, proj, up, down,
    ex, ea, eu, ey, egp, eqkv, ep, eo, ex1, epart, esend, erecv, esend2, erecv2, eown,
    cot, x0, x1, a, acts, probs, o, inverse, u, ut, y, gp, g32, gb, gt, acc, e_ref, hot, perm, buf, dsend, e_rc, e_rcy, e_ry,
    load_s, out_s, cot_s, w_s, w_r, bias_s, bias_r, dw_s, dw_r, ex_s, ex_r, ex2_s, ex2_r, do_s, do_r, e_s, e_r,
):
    sec = lax.axis_index("section")
    lane = lax.axis_index("tensor")
    mate = lane + 1 - 2 * lax.rem(lane, 2)
    over = lax.rem(lane + 2, LANES)
    cross = lax.rem(mate + 2, LANES)
    me = sec * LANES + lane
    devices = 2 * LANES
    clip = me
    clips = (me, sec * LANES + over)

    def group_peer(step):
        peer = lax.rem(me + step, devices)
        return peer, {"section": lax.div(peer, LANES), "tensor": lax.rem(peer, LANES)}

    own = [
        pltpu.make_async_copy(src, dst.at[0], load_s.at[n])
        for n, (src, dst) in enumerate(
            ((h_qkv, w_qkv), (h_proj, w_proj), (h_up, w_up), (h_down, w_down))
        )
    ]

    def place(n, shard, part=None):
        thick = (128, 128, 512, 512)[n]
        base = shard * thick
        cut = pl.ds(pl.multiple_of(base, thick), thick)
        if part is None:
            return (qkv.at[:, :, cut], proj.at[cut, :], up.at[:, cut], down.at[cut, :])[n]
        some = span(part, (256, 64, 256, 256)[n])
        if n == 0:
            return qkv.at[:, some, cut]
        if n == 2:
            return up.at[some, cut]
        few = thick // 2
        rows = pl.ds(pl.multiple_of(base + part * few, few), few)
        return (proj if n == 1 else down).at[rows, :]

    shards = (h_dqkv, h_dproj, h_dup, h_ddown)
    keep = [
        pltpu.make_async_copy(shards[n], place(n, lane), load_s.at[4 + n]) for n in range(4)
    ]
    for copy in own + keep:
        copy.start()
    fetch = pltpu.make_async_copy(cot_hbm.at[clip], cot, cot_s)
    fetch.start()

    barrier = pltpu.get_barrier_semaphore()
    for step in range(1, devices):
        pl.semaphore_signal(barrier, inc=1, device_id_type=MESH, device_id=group_peer(step)[1])
    bias[...] = jnp.zeros_like(bias)
    half = w_proj.shape[1]
    bias[0:1, :] = b_up[...].astype(F32).reshape(1, -1)
    bias[1:3, 0:half] = b_qv[...].astype(F32)
    bias[3:4, 0:512] = b_dup[...].astype(F32).reshape(1, -1)
    bias[4:6, 0:128] = b_dqv[...].astype(F32)
    biases[lane] = bias[...]
    pl.semaphore_wait(barrier, devices - 1)

    def enc_weight(n):
        src = (h_qkv, h_proj, h_up, h_down)[n]
        dst = (w_qkv, w_proj, w_up, w_down)[n]
        return far(src, dst.at[1], w_s.at[n], w_r.at[n], {"tensor": mate})

    def bias_copy(step):
        return far(
            bias, biases.at[lane], bias_s.at[step], bias_r.at[step],
            {"tensor": lax.rem(lane + step, LANES)},
        )

    def half_of(n):
        some = span(sec, (256, 64, 256, 256)[n])
        return shards[n].at[:, some, :] if n == 0 else shards[n].at[some, :]

    def dec_weight(n, kind):
        peer = {"section": 1 - sec} if kind == 2 else {"tensor": over if kind == 0 else mate}
        if kind == 0:
            src, dst = half_of(n), place(n, lane, sec)
        elif kind == 1:
            src, dst = shards[n], place(n, lane)
        else:
            src = dst = place(n, over, 1 - sec if kind == 4 else sec)
        return far(src, dst, dw_s.at[5 * n + kind], dw_r.at[5 * n + kind], peer)

    enc_weight(0).start()
    for step in range(1, LANES):
        bias_copy(step).start()
    enc_weight(1).start()
    dec_weight(0, 0).start()
    enc_weight(2).start()
    enc_weight(3).start()
    for n in range(4):
        dec_weight(n, 1).start()

    def pass_on(n):
        dec_weight(n, 0).wait_recv()
        dec_weight(n, 2).start()
        dec_weight(n, 3).start()

    def pass_last(n):
        dec_weight(n, 2).wait_recv()
        dec_weight(n, 4).start()

    def arrived(n):
        keep[n].wait()
        dec_weight(n, 1).wait_recv()
        dec_weight(n, 3).wait_recv()
        dec_weight(n, 4).wait_recv()

    width = wid[clip]
    bits = jnp.where(width == WIDE, 3, 2)
    turn = shifts[0, clip] * width
    mod = GRID - 1
    spot = 0
    for i in range(order.shape[1]):
        spot = spot + jnp.where(order[0, i] == clip, i, 0)
    batch = spot // CM
    count = 0
    for i in range(order.shape[1]):
        count = count + jnp.where(batch == i // CM, wid[order[0, i]], 0)
    factor_rows = CM * GRID / (jnp.full((1, 1), count, jnp.int32) * GRID_ROWS).astype(F32)

    def slot_of(index):
        return (index - turn) & mod

    def code_of(slot):
        band = ((slot >> bits) + shifts[0, clip]) >> 2
        strip = ((slot & (width - 1)) + shifts[1, clip]) >> 2
        return band * 4 + strip

    def valid_rows():
        slot = slot_of(lax.broadcasted_iota(jnp.int32, (GRID, 1), 0))
        return (slot < GRID_ROWS * width).astype(F32)

    def clip_gradient():
        fetch.wait()
        rolled = slot_of(lax.broadcasted_iota(jnp.int32, (GRID, GRID), 0))
        column = lax.broadcasted_iota(jnp.int32, (GRID, GRID), 1)
        perm[...] = (rolled == column).astype(F32).astype(BF16)
        g = nn(perm[...], cot[...]) * valid_rows() * factor_rows
        g32[...] = g
        gb[...] = g.astype(BF16)
        gt[...] = jnp.transpose(g).astype(BF16)
        d_small[...] = jnp.zeros_like(d_small)
        d_small[5:6, :] = colsum(g)

    seen = vis[pl.ds(clip, 1), :]
    target = jnp.concatenate([(seen + turn) & mod, jnp.full((1, PAD - VIS), -1, jnp.int32)], 1)

    def places(i):
        r = span(i, PAD)
        index = lax.broadcasted_iota(jnp.int32, (PAD, PAD), 0) + i * PAD
        column = lax.broadcasted_iota(jnp.int32, (PAD, PAD), 1)
        hot[r, :] = (index == target).astype(F32).astype(BF16)
        slot = slot_of(index)
        by_row = ((slot >> bits) == column).astype(F32).astype(BF16)
        by_col = ((slot & (width - 1)) == column).astype(F32).astype(BF16)
        row_part = nn(by_row, table[0]) + nn(by_row, table[1])
        col_part = nn(by_col, table[0]) + nn(by_col, table[1])
        x0[r, :] = jnp.concatenate([row_part, col_part], 1)

    egain = gains[...].astype(F32)
    eoff = offs[...].astype(F32)
    stride = pat.shape[0] // VIS
    for c in range(2):
        row = lax.broadcasted_iota(jnp.int32, (PAD, pat.shape[0]), 0)
        col = lax.broadcasted_iota(jnp.int32, (PAD, pat.shape[0]), 1)
        pick = (col == row * stride + clips[c]).astype(F32).astype(BF16)
        ex[c * PAD : (c + 1) * PAD, :] = nn(pick, pat[...])

    emarks = head_marks(half, ENC_SIZE, BF16)
    key = lax.broadcasted_iota(jnp.int32, (PAD, PAD), 1)
    floor = jnp.where(key < VIS, NEG * LOG2E, -1e30)
    eones = ones_per_head(PAD, emarks)
    blocks = D // 256

    def give_part(i, side):
        cut = span(i, 256)
        return far(
            esend.at[(1 - side) * PAD : (2 - side) * PAD, cut],
            erecv.at[side * PAD : (side + 1) * PAD, cut],
            ex_s.at[2 * i + side], ex_r.at[2 * i + side], {"tensor": over},
        )

    for c in range(2):
        rows = slice(c * PAD, (c + 1) * PAD)
        hat, _ = normal(ex[rows, :])
        ea[rows, :] = (hat * egain[0:1] + eoff[0:1]).astype(BF16)
        limit = (VIS * wid[clips[c]]) // WIDE
        for g, shard in enumerate((lane, mate)):
            if c == 0 and g == 0:
                own[0].wait()
            if c == 0 and g == 1:
                enc_weight(0).wait_recv()
                for step in range(1, LANES):
                    bias_copy(step).wait_recv()
            if g == 0:
                bq, bv = bias[1:2, 0:half], bias[2:3, 0:half]
            else:
                bq, bv = biases[shard, 1:2, 0:half], biases[shard, 2:3, 0:half]
            eqkv[g, 0, rows] = (nt(ea[rows, :], w_qkv[g, 0]) + bq).astype(BF16)
            eqkv[g, 1, rows] = nt(ea[rows, :], w_qkv[g, 1]).astype(BF16)
            eqkv[g, 2, rows] = (nt(ea[rows, :], w_qkv[g, 2]) + bv).astype(BF16)
            p, out, _ = attend(
                eqkv[g, 0, rows], eqkv[g, 1, rows], eqkv[g, 2, rows], emarks, eones,
                lambda s: jnp.where(key < limit, s, floor), ENC_SCALE,
            )
            ep[g, c] = p
            eo[g, rows] = out
        if c == 0:
            own[1].wait()
            enc_weight(1).wait_recv()
        for i in range(blocks):
            cut = slice(i * 256, (i + 1) * 256)
            t = nn(eo[0, rows], w_proj[0, :, cut]) + nn(eo[1, rows], w_proj[1, :, cut])
            epart[rows, cut] = t
            esend[rows, cut] = t.astype(BF16)
            give_part(i, 1 - c).start()
    pass_on(0)
    clip_gradient()
    own[2].wait()
    enc_weight(2).wait_recv()

    def give_last(i):
        cut = span(i, 256)
        return far(
            esend2.at[:, cut], erecv2.at[:, cut], ex2_s.at[i], ex2_r.at[i], {"tensor": over}
        )

    for c in (1, 0):
        rows = slice(c * PAD, (c + 1) * PAD)
        for i in range(blocks):
            give_part(i, c).wait_recv()
        t = ex[rows, :] + epart[rows, :] + erecv[rows, :].astype(F32) + eoff[2:3]
        ex1[rows, :] = t
        hat, _ = normal(t)
        eu[rows, :] = (hat * egain[1:2] + eoff[1:2]).astype(BF16)
        for g, shard in enumerate((lane, mate)):

            def enc_ff(i, g=g, shard=shard, rows=rows):
                cut = span(i, 256)
                h = nn(eu[rows, :], w_up[g, :, cut]) + biases[shard, 0:1, cut]
                act, slope = gelu_both(h)
                ey[g, rows, cut] = act.astype(BF16)
                egp[g, rows, cut] = slope.astype(BF16)

            loop(w_up.shape[2] // 256, enc_ff, unroll=3)
        if c == 1:
            own[3].wait()
            enc_weight(3).wait_recv()
        for i in range(blocks):
            cut = slice(i * 256, (i + 1) * 256)
            t = nn(ey[0, rows], w_down[0, :, cut]) + nn(ey[1, rows], w_down[1, :, cut])
            if c == 0:
                eown[:, cut] = t
            else:
                esend2[:, cut] = t.astype(BF16)
                give_last(i).start()
        if c == 1:
            for n in (1, 2, 3):
                dec_weight(n, 0).start()
            pass_last(0)
    outs = [
        pltpu.make_async_copy(src, dst, out_s.at[n])
        for n, (src, dst) in enumerate(
            (
                (ex.at[0:PAD, :], o_x), (ex1, o_x1), (ea, o_a), (eu, o_u), (ey, o_y), (egp, o_gp),
                (eqkv, o_qkv), (ep, o_p), (eo, o_o), (w_qkv.at[1], o_w), (w_proj.at[1], o_wproj),
                (w_up.at[1], o_wup), (w_down.at[1], o_wdown),
            )
        )
    ]
    for copy in outs:
        copy.start()
    loop(GRID // PAD, places, unroll=2)
    for i in range(blocks):
        give_last(i).wait_recv()

    e_ref[...] = (ex1[0:PAD, :] + eown[...] + erecv2[...].astype(F32) + eoff[3:4]).astype(BF16)
    vec = evec[...].astype(F32)
    m = (nn(e_ref[...], ew[...]) + vec[0:1]).astype(BF16)
    gain = dgains[...].astype(F32)
    offsets = doffs[...].astype(F32)

    def start(i):
        r = span(i, PAD)
        oh = hot[r, :]
        hit = jnp.sum(oh.astype(F32), -1, keepdims=True)
        x = jnp.where(hit > 0, nn(oh, m), vec[1:2]).astype(BF16).astype(F32) + x0[r, :]
        x0[r, :] = x
        hat, _ = normal(x)
        a[r, :] = (hat * gain[0:1] + offsets[0:1]).astype(BF16)

    loop(GRID // PAD, start, unroll=2)
    arrived(0)

    def dec_bias(row, size):
        return jnp.concatenate([biases[k, row : row + 1, 0:size] for k in range(LANES)], 1)

    def project(i):
        r = span(i, 256)
        rows = a[r, :]
        acts[0, r, :] = (nn(rows, qkv[0]) + dec_bias(4, 128)).astype(BF16)
        acts[1, r, :] = nn(rows, qkv[1]).astype(BF16)
        acts[2, r, :] = (nn(rows, qkv[2]) + dec_bias(5, 128)).astype(BF16)

    loop(2, project)
    pass_on(1)
    pass_on(2)
    marks = head_marks(128, DEC_SIZE, BF16)
    marks32 = head_marks(128, DEC_SIZE, F32)
    dim = lax.broadcasted_iota(jnp.int32, (128, 1), 0)
    rows32 = [
        ((dim >= h * DEC_SIZE) & (dim < (h + 1) * DEC_SIZE)).astype(F32) for h in range(len(marks))
    ]

    ones = ones_per_head(PAD, marks)

    def attention(i):
        r = span(i, PAD)
        row_slot = slot_of(lax.broadcasted_iota(jnp.int32, (PAD, PAD), 0) + i * PAD)
        key_slot = slot_of(lax.broadcasted_iota(jnp.int32, (PAD, PAD), 1) + i * PAD)
        allowed = (code_of(row_slot) == code_of(key_slot)) & (key_slot < GRID_ROWS * width)
        for g in range(DD // 128):
            c = slice(g * 128, (g + 1) * 128)
            probs[i, :, g * 512 : (g + 1) * 512], o[r, c], inverse[r, c] = attend(
                acts[0, r, c], acts[1, r, c], acts[2, r, c], marks, ones,
                lambda s: jnp.where(allowed, s, NEG * LOG2E), DEC_SCALE,
            )

    loop(GRID // PAD, attention, unroll=2)
    pass_last(1)
    pass_last(2)
    pass_on(3)
    arrived(1)

    def mix(i):
        r = span(i, PAD)
        x = x0[r, :] + nn(o[r, :], proj[...]) + offsets[2:3]
        x1[r, :] = x
        hat, _ = normal(x)
        un = hat * gain[1:2] + offsets[1:2]
        u[r, :] = un.astype(BF16)
        ut[:, r] = jnp.transpose(un).astype(BF16)

    loop(GRID // PAD, mix, unroll=2)
    pass_last(3)
    arrived(2)

    def ff(i):
        k = lax.div(i, 4)
        side = lax.rem(lax.div(i, 2), 2)
        c = span(lax.div(i, 2), 256)
        r = span(lax.rem(i, 2), 256)
        h = nn(u[r, :], up[:, c]) + biases[k, 3:4, span(side, 256)]
        act, slope = gelu_both(h)
        y[r, c] = act.astype(BF16)
        gp[r, c] = slope.astype(BF16)

    loop(2 * up.shape[1] // 256, ff, unroll=2)
    arrived(3)
    def out(i):
        r = span(lax.rem(i, 2), 256)
        c = span(lax.div(i, 2), 256)
        acc[r, c] = nn(y[r, :], down[:, c])

    loop(4, out, unroll=2)
    full = ((acc[...] + x1[...] + offsets[3:4]) * valid_rows()).astype(BF16)
    turned = tn(full, perm[...]).astype(BF16)
    for k in range(devices):
        dsend[k] = turned[k * dsend.shape[1] : (k + 1) * dsend.shape[1]]

    def decoded_copy(step):
        peer, spot = group_peer(step)
        return far(dsend.at[peer], dec_out.at[me], do_s.at[step], do_r.at[step], spot)

    for step in range(1, devices):
        decoded_copy(step).start()
    dec_out[me] = dsend[me]

    def ff_back(shard):
        for side in range(2):
            c = span(2 * shard + side, 256)
            d_down = nn(gt[...], y[:, c]).astype(BF16)
            dh = nt(gb[...], down[c, :]) * gp[:, c].astype(F32)
            d_upb[:, c] = colsum(dh)
            du = dh.astype(BF16)
            gp[:, c] = du
            d_up = nn(ut[...], du).astype(BF16)
            for block in range(GRID // CH):
                rows = slice(block * CH, (block + 1) * CH)
                h, top, col = tile_of(4 * block + side)
                buf[shard, h, top : top + CH, col : col + 256] = d_up[rows]
                h, top, col = tile_of(4 * block + 2 + side)
                buf[shard, h, top : top + CH, col : col + 256] = d_down[rows]

    def early_core(which):
        shard, land = ((mate, e_rc), (cross, e_rcy))[which]
        return far(
            buf.at[shard, :, 0:EARLY_ROWS, :], land, e_s.at[which], e_r.at[which], {"tensor": mate}
        )

    def early_y():
        return far(
            buf.at[over, :, 0:EARLY_ROWS, :], e_ry, e_s.at[2], e_r.at[2], {"tensor": over}
        )

    def early_add(shard, land):
        def body(i):
            r = span(i, CH)
            buf[shard, :, r, :] = buf[shard, :, r, :] + land[:, r, :]

        loop(EARLY_ROWS // CH, body)

    def ff_step(i):
        ff_back(jnp.where(i == 0, cross, jnp.where(i == 1, over, jnp.where(i == 2, mate, lane))))

        @pl.when(i == 1)
        def _():
            early_core(1).start()

        @pl.when(i == 2)
        def _():
            early_core(0).start()
            early_core(1).wait_recv()
            early_add(over, e_rcy)
            early_y().start()

    loop(LANES, ff_step)

    def ff_in(i):
        r = span(lax.rem(i, 2), 256)
        c = span(lax.div(i, 2), 256)
        acc[r, c] = nt(gp[r, :], up[c, :])

    loop(4, ff_in, unroll=2)

    def mix_back(i):
        r = span(i, PAD)
        hat, scale = normal(x1[r, :])
        da = acc[r, :]
        dx = g32[r, :] + normal_back(da, hat, scale, gain[1:2])
        d_small[1:2, :] += colsum(da * hat)
        d_small[3:4, :] += colsum(da)
        d_small[4:5, :] += colsum(dx)
        g32[r, :] = dx
        dxb = dx.astype(BF16)
        gb[r, :] = dxb
        u[r, :] = nt(dxb, proj[...]).astype(BF16)

    loop(GRID // PAD, mix_back, unroll=2)
    early_core(0).wait_recv()
    early_add(lane, e_rc)
    d_proj = tn(o[...], gb[...]).astype(BF16)
    for block in range(GRID // CH):
        h, top, col = tile_of(33 + 2 * block)
        side = slice(block // 2 * 128, (block // 2 + 1) * 128)
        for k in range(LANES):
            row = k * 128 + block % 2 * CH
            buf[k, h, top : top + CH, col + 128 : col + 256] = d_proj[row : row + CH, side]

    def attention_back(i):
        r = span(i, PAD)
        for k in range(DD // 128):
            c = slice(k * 128, (k + 1) * 128)
            acts[0, r, c], acts[1, r, c], acts[2, r, c] = attend_back(
                acts[0, r, c], acts[1, r, c], acts[2, r, c],
                probs[i, :, k * 512 : (k + 1) * 512], o[r, c], inverse[r, c], u[r, c],
                marks, marks32, rows32, ones, DEC_SCALE,
            )

    loop(GRID // PAD, attention_back, unroll=2)
    d_qvb[0:1, :] = colsum(acts[0].astype(F32))
    d_qvb[1:2, :] = colsum(acts[2].astype(F32))

    def project_back(i):
        r = span(lax.rem(i, 2), 256)
        c = span(lax.div(i, 2), 256)
        acc[r, c] = (
            nt(acts[0, r, :], qkv[0, c, :])
            + nt(acts[1, r, :], qkv[1, c, :])
            + nt(acts[2, r, :], qkv[2, c, :])
        )

    loop(4, project_back, unroll=2)
    gt[...] = jnp.transpose(a[...].astype(F32)).astype(BF16)
    for j in range(3):
        d_qkv = nn(gt[...], acts[j]).astype(BF16)
        for block in range(GRID // CH):
            h, top, col = tile_of(32 + 2 * block + j // 2)
            col = col + j % 2 * 128
            rows = slice(block * CH, (block + 1) * CH)
            for k in range(LANES):
                buf[k, h, top : top + CH, col : col + 128] = d_qkv[rows, k * 128 : (k + 1) * 128]

    def start_back(i):
        r = span(i, PAD)
        hat, scale = normal(x0[r, :])
        da = acc[r, :]
        dx = g32[r, :] + normal_back(da, hat, scale, gain[0:1])
        d_small[0:1, :] += colsum(da * hat)
        d_small[2:3, :] += colsum(da)
        dg = dx.astype(BF16)
        gb[r, :] = dg
        hit = jnp.sum(hot[r, :].astype(F32), -1, keepdims=True)
        d_small[7:8, :] += colsum(jnp.where(hit > 0, 0.0, dg.astype(F32)))

    loop(GRID // PAD, start_back, unroll=2)
    dm = tn(hot[...], gb[...])
    d_small[6:7, :] = colsum(dm)
    dmb = dm.astype(BF16)
    d_enc[...] = nt(dmb, ew[...]).astype(BF16)
    d_ew = tn(e_ref[...], dmb).astype(BF16)
    for k in range(LANES):
        for h in range(2):
            top = k * 192 + h * 64
            buf[k, h, 512:576, 0:512] = d_ew[top : top + 64]
            buf[k, h, 512:576, 512:768] = d_ew[k * 192 + 128 : (k + 1) * 192, h * 256 : (h + 1) * 256]

    early_y().wait_recv()
    early_add(lane, e_ry)
    later = pl.ds(EARLY_ROWS, DEC_ROWS - EARLY_ROWS)
    rest = [pltpu.make_async_copy(buf.at[lane], o_dec.at[lane], out_s.at[13])] + [
        pltpu.make_async_copy(buf.at[k, :, later, :], o_dec.at[k, :, later, :], out_s.at[14 + n])
        for n, k in enumerate((mate, over, cross))
    ]
    for copy in rest:
        copy.start()
    for copy in outs + rest:
        copy.wait()
    for which in range(2):
        early_core(which).wait_send()
    early_y().wait_send()
    for n in range(4):
        enc_weight(n).wait_send()
        for kind in range(5):
            dec_weight(n, kind).wait_send()
    for step in range(1, LANES):
        bias_copy(step).wait_send()
    for i in range(blocks):
        give_part(i, 0).wait_send()
        give_part(i, 1).wait_send()
        give_last(i).wait_send()
    for step in range(1, devices):
        decoded_copy(step).wait()


def forward_call(args, half, hid, dff):
    dma = lambda *s: pltpu.SemaphoreType.DMA(s)
    vm = lambda dtype, *shape: pltpu.VMEM(shape, dtype)
    rows = 2 * PAD
    keys = PAD * half // ENC_SIZE
    devices = 2 * LANES
    slab = DD // devices
    kept = [
        ((PAD, D), F32), ((rows, D), F32), ((rows, D), BF16), ((rows, D), BF16),
        ((2, rows, hid), BF16), ((2, rows, hid), BF16), ((2, 3, rows, half), BF16),
        ((2, 2, PAD, keys), BF16), ((2, rows, half), BF16),
        ((3, half, D), BF16), ((half, D), BF16), ((D, hid), BF16), ((hid, D), BF16),
        ((LANES, 2, DEC_ROWS, D), BF16),
    ]
    made = [
        ((PAD, D), BF16), ((2, DD), F32), ((1, dff), F32), ((8, DD), F32),
        ((devices, slab, GRID), BF16),
    ]
    return pl.pallas_call(
        forward_and_decoder,
        out_shape=[jax.ShapeDtypeStruct(s, d) for s, d in kept + made],
        in_specs=[SM, SM, SM] + [VM] * 8 + [ANY] * 9 + [VM] * 5,
        out_specs=[ANY] * len(kept) + [VM] * len(made),
        scratch_shapes=[
            vm(BF16, 2, 3, half, D), vm(BF16, 2, half, D), vm(BF16, 2, D, hid), vm(BF16, 2, hid, D),
            vm(F32, 8, D), vm(F32, LANES, 8, D),
            vm(BF16, 3, DD, DD), vm(BF16, DD, DD), vm(BF16, DD, dff), vm(BF16, dff, DD),
            vm(F32, rows, D), vm(BF16, rows, D), vm(BF16, rows, D), vm(BF16, 2, rows, hid),
            vm(BF16, 2, rows, hid), vm(BF16, 2, 3, rows, half), vm(BF16, 2, 2, PAD, keys),
            vm(BF16, 2, rows, half), vm(F32, rows, D), vm(F32, rows, D), vm(BF16, rows, D),
            vm(BF16, rows, D), vm(BF16, PAD, D), vm(BF16, PAD, D), vm(F32, PAD, D),
            vm(BF16, GRID, DD), vm(F32, GRID, DD), vm(F32, GRID, DD), vm(BF16, GRID, DD),
            vm(BF16, 3, GRID, DD), vm(BF16, GRID // PAD, PAD, DHEADS * PAD), vm(BF16, GRID, DD),
            vm(F32, GRID, DD),
            vm(BF16, GRID, DD), vm(BF16, DD, GRID), vm(BF16, GRID, dff), vm(BF16, GRID, dff),
            vm(F32, GRID, DD), vm(BF16, GRID, DD), vm(BF16, DD, GRID), vm(F32, GRID, DD),
            vm(BF16, PAD, D), vm(BF16, GRID, PAD), vm(BF16, GRID, GRID),
            vm(BF16, LANES, 2, DEC_ROWS, D),
            vm(BF16, devices, slab, GRID), *[vm(BF16, 2, EARLY_ROWS, D)] * 3,
            dma(8), dma(17), pltpu.SemaphoreType.DMA, dma(4), dma(4), dma(LANES), dma(LANES),
            dma(20), dma(20), dma(6), dma(6), dma(3), dma(3), dma(devices), dma(devices),
            dma(3), dma(3),
        ],
        compiler_params=pltpu.CompilerParams(
            collective_id=0, has_side_effects=True, vmem_limit_bytes=VMEM_LIMIT
        ),
    )(*args)


def add(x, y):
    return x + y


def backward_and_sums(
    d_enc, gains,
    h_u, h_y, h_gp, h_down0, h_down1, h_up0, h_up1,
    h_x, h_x1, h_a, h_qkv, h_p, h_o, h_w0, h_w1, h_proj0, h_proj1,
    dec, dec_qvb, dec_upb, dec_small,
    out, emb, dx_out,
    gb, gt, ut, part, send, recv, du, gx, dx1, d_o, d_acts, own, send1, recv1, dx32, dx,
    d_upb, d_qvb, d_small,
    acc, yacc, enc_mate, rcy, ry, rx, zl, zr, xc, cl, cr, small32, small,
    u, y, gp, down0, down1, up0, up1, x, x1, a, qkv, p, o, w0, w1, proj0, proj1, fetch_s,
    load_s, ex_s, ex_r,
    core_s, core_r, corey_s, corey_r, y_s, y_r, x_s, x_r, z_s, zl_r, zr_r,
    bl_s, br_s, b_r, a_s, a_r, emb_s, emb_r, dx_s, dx_r,
):
    sec = lax.axis_index("section")
    lane = lax.axis_index("tensor")
    pos = lax.axis_index("dp")
    count = lax.axis_size("dp")
    mate = lane + 1 - 2 * lax.rem(lane, 2)
    over = lax.rem(lane + 2, LANES)
    cross = lax.rem(mate + 2, LANES)
    first = pos == 0
    last = pos == count - 1
    me = sec * LANES + lane
    devices = 2 * LANES

    def group_peer(step):
        peer = lax.rem(me + step, devices)
        return peer, {"section": lax.div(peer, LANES), "tensor": lax.rem(peer, LANES)}

    barrier = pltpu.get_barrier_semaphore()
    for step in range(1, devices):
        pl.semaphore_signal(barrier, inc=1, device_id_type=MESH, device_id=group_peer(step)[1])

    @pl.when(pos > 0)
    def _():
        pl.semaphore_signal(barrier, inc=1, device_id={"dp": pos - 1}, device_id_type=MESH)

    @pl.when(pos < count - 1)
    def _():
        pl.semaphore_signal(barrier, inc=1, device_id={"dp": pos + 1}, device_id_type=MESH)

    fetches = [
        pltpu.make_async_copy(src, dst, fetch_s.at[n])
        for n, (src, dst) in enumerate(
            (
                (h_u, u), (h_y, y), (h_gp, gp), (h_down0, down0), (h_down1, down1), (h_up0, up0),
                (h_up1, up1), (h_x, x), (h_x1, x1), (h_a, a), (h_qkv, qkv), (h_p, p), (h_o, o),
                (h_w0, w0), (h_w1, w1), (h_proj0, proj0), (h_proj1, proj1),
            )
        )
    ]
    for fetch in fetches:
        fetch.start()
    loads = [
        pltpu.make_async_copy(dec.at[lane], acc.at[:, 0:DEC_ROWS, :], load_s.at[0]),
        pltpu.make_async_copy(
            dec.at[over, :, EARLY_ROWS:DEC_ROWS, :], yacc.at[:, 0 : DEC_ROWS - EARLY_ROWS, :],
            load_s.at[1],
        ),
    ]
    for load in loads:
        load.start()
    small32[...] = jnp.zeros_like(small32)
    small[...] = jnp.zeros_like(small)
    d_small[...] = jnp.zeros_like(d_small)
    gb[0:PAD, :] = d_enc[...]
    ends = jnp.where(first, 0, 1) + jnp.where(last, 0, 1)
    pl.semaphore_wait(barrier, devices - 1 + ends)

    gain = gains[...].astype(F32)
    width = w0.shape[1]
    marks = head_marks(width, ENC_SIZE, BF16)
    marks32 = head_marks(width, ENC_SIZE, F32)
    ones = ones_per_head(PAD, marks)

    def rows(k, size=CH):
        return pl.ds(pl.multiple_of(k * size, size), size)

    def give_enc():
        return far(d_enc, gb.at[PAD : 2 * PAD, :], ex_s.at[0], ex_r.at[0], {"tensor": over})

    def give_part(i, half):
        cut = rows(i, 256)
        n = 1 + 2 * i + half
        return far(
            send.at[(1 - half) * PAD : (2 - half) * PAD, cut],
            recv.at[half * PAD : (half + 1) * PAD, cut],
            ex_s.at[n], ex_r.at[n], {"tensor": over},
        )

    def give_last(i):
        cut = rows(i, 256)
        return far(send1.at[:, cut], recv1.at[:, cut], ex_s.at[7 + i], ex_r.at[7 + i], {"tensor": over})

    def ff_back(g, i, down):
        c = rows(i, 256)
        d_down = nn(gt[...], y[g, :, c]).astype(BF16)
        dh = nt(gb[...], down[c, :]) * gp[g, :, c].astype(F32)
        d_upb[g, :, c] = colsum(dh)
        dub = dh.astype(BF16)
        du[g, :, c] = dub
        d_up = nn(ut[...], dub).astype(BF16)
        if g == 0:
            acc[1, A_TOP:B_TOP, c] = d_down
            acc[0, A_TOP:B_TOP, c] = d_up
        else:
            enc_mate[1, 0:ENC_A, c] = d_down
            enc_mate[0, 0:ENC_A, c] = d_up

    def ff_in(i):
        c = rows(i, 256)
        t = nt(du[0], up0[c, :]) + nt(du[1], up1[c, :])
        part[:, c] = t
        send[:, c] = t.astype(BF16)
        give_part(i, 0).start()
        give_part(i, 1).start()

    def norm_two(i):
        del i
        for fetch in fetches[7:]:
            fetch.wait()
        for k in range(D // 256):
            give_part(k, 0).wait_recv()
            give_part(k, 1).wait_recv()

        def body(j):
            r = rows(j, 64)
            da = part[r, :] + recv[r, :].astype(F32)
            hat, scale = normal(x1[r, :])
            g = gb[r, :].astype(F32)
            d = g + normal_back(da, hat, scale, gain[1:2])
            gx[r, :] = d.astype(BF16)
            dx1[r, :] = d

            @pl.when(j < 2)
            def _():
                d_small[1:2, :] += colsum(da * hat)
                d_small[3:4, :] += colsum(da)
                d_small[4:5, :] += colsum(d)
                d_small[5:6, :] += colsum(g)

        loop(2 * PAD // 64, body)

    def attention(g, proj):
        d_proj = tn(o[g], gx[...]).astype(BF16)
        if g == 0:
            acc[1, B_TOP + width : S_TOP, :] = d_proj
        else:
            enc_mate[1, ENC_A + width : ENC_A + 2 * width, :] = d_proj
        d_o[...] = nt(gx[...], proj[...]).astype(BF16)
        for c in range(2):
            r = slice(c * PAD, (c + 1) * PAD)
            dq, dk, dv = attend_back(
                qkv[g, 0, r], qkv[g, 1, r], qkv[g, 2, r], p[g, c], o[g, r], 1.0 / nn(p[g, c], ones),
                d_o[r, :], marks, marks32, None, ones, ENC_SCALE,
            )
            d_acts[g, 0, r] = dq
            d_acts[g, 1, r] = dk
            d_acts[g, 2, r] = dv
        d_qvb[g, 0:1, :] = colsum(d_acts[g, 0].astype(F32))
        d_qvb[g, 1:2, :] = colsum(d_acts[g, 2].astype(F32))

    def project_in(i):
        c = rows(i, 256)
        t = 0.0
        for g, w in enumerate((w0, w1)):
            for j in range(3):
                t += nn(d_acts[g, j], w[j, :, c])
        own[:, c] = t[:PAD]
        send1[:, c] = t[PAD:].astype(BF16)
        give_last(i).start()

    def project_grad(g):
        for j in range(3):
            row = (j % 2) * width
            d = tn(d_acts[g, j], a[...]).astype(BF16)
            if g == 0:
                acc[j // 2, B_TOP + row : B_TOP + row + width, :] = d
            else:
                enc_mate[j // 2, ENC_A + row : ENC_A + row + width, :] = d

    def norm_one(i):
        del i
        for k in range(D // 256):
            give_last(k).wait_recv()

        def body(j):
            r = rows(j, 64)
            da = own[r, :] + recv1[r, :].astype(F32)
            hat, scale = normal(x[r, :])
            d_small[0:1, :] += colsum(da * hat)
            d_small[2:3, :] += colsum(da)
            dx32[r, :] = dx1[r, :] + normal_back(da, hat, scale, gain[0:1])

        loop(PAD // 64, body)
        turned = jnp.transpose(dx32[...])
        cut = D // devices
        for k in range(devices):
            dx[k] = turned[k * cut : (k + 1) * cut, 0:VIS].astype(BF16)
        for r in range(LANES):
            small32[r, 0:1, 0:512] = dec_upb[:, r * 512 : (r + 1) * 512]
            small32[r, 1:2, 0:128] = dec_qvb[0:1, r * 128 : (r + 1) * 128]
            small32[r, 1:2, 128:256] = dec_qvb[1:2, r * 128 : (r + 1) * 128]
            small32[r, 8:16, 0:512] = dec_small[...]
            small32[r, 16:24, :] = d_small[...]
        for g, shard in enumerate((lane, mate)):
            small32[shard, 2:3, :] = d_upb[g]
            small32[shard, 3:4, 0:192] = d_qvb[g, 0:1]
            small32[shard, 3:4, 256:448] = d_qvb[g, 1:2]
        for r in range(LANES):
            small[r, 0, 0:32] = small32[r].astype(BF16)
        acc[:, S_TOP : S_TOP + CH, :] = small[lane]
        yacc[:, DEC_ROWS - EARLY_ROWS :, :] = small[over]
        core_copy(LATE, small.at[mate]).start()
        corey_copy(LATE, small.at[cross]).start()
        for step in range(1, devices):
            dx_copy(step).start()
        dx_out[me] = dx[me]

    def core_enc(lo, hi):
        def body(m):
            block = block_of(m)

            @pl.when((block >= lo) & (block < hi))
            def _():
                src = pl.ds(pl.multiple_of(block * CH - DEC_ROWS, CH), CH)
                core_copy(m, enc_mate.at[:, src, :]).start()

        loop(ALL_K, body)

    def first_piece(i):
        del i
        for fetch in fetches[:7]:
            fetch.wait()
        ut[...] = jnp.transpose(u[...].astype(F32)).astype(BF16)
        give_enc().wait_recv()
        gt[...] = jnp.transpose(gb[...].astype(F32)).astype(BF16)

    pieces = [(WAIT, WAIT + 1, first_piece)]
    for g, down in enumerate((down0, down1)):
        pieces.append((WAIT, WAIT + 3, lambda i, g=g, down=down: ff_back(g, i, down)))
    pieces.append((WAIT + 3, WAIT + 4, lambda i: core_enc(DEC_K, DEC_K + ENC_A // CH)))
    pieces.append((WAIT + 3, WAIT + 4, lambda i: loop(D // 256, ff_in)))
    pieces.append((WAIT + 6, WAIT + 7, norm_two))
    for g, proj in enumerate((proj0, proj1)):
        low = WAIT + 7 + g
        pieces.append((low, low + 1, lambda i, g=g, proj=proj: attention(g, proj)))
    pieces.append((WAIT + 9, WAIT + 10, lambda i: loop(D // 256, project_in)))
    for g in range(2):
        low = WAIT + 10 + g
        pieces.append((low, low + 1, lambda i, g=g: project_grad(g)))
    pieces.append((WAIT + 12, WAIT + 13, lambda i: core_enc(DEC_K + ENC_A // CH, B_K)))
    pieces.append((WAIT + 13, WAIT + 14, norm_one))

    def dx_copy(step):
        peer, place = group_peer(step)
        return far(dx.at[peer], dx_out.at[me], dx_s.at[step], dx_r.at[step], place)

    def emb_copy(step):
        return far(
            out.at[:, pl.ds(512, CH), :], emb.at[lane], emb_s.at[step], emb_r.at[step],
            {"tensor": lax.rem(lane + step, LANES)},
        )

    def block_of(m):
        even = lax.rem(m - EARLY, 2) == 0
        turn = jnp.where(even, EARLY + lax.div(m - EARLY, 2), DEC_K + lax.div(m - EARLY - 1, 2))
        late = jnp.where(m == LATE, ALL_K - 1, jnp.where(m > LATE, m - 1, m))
        return jnp.where(m < EARLY, m, jnp.where(m >= MIXED, late, turn))

    def is_dec(m):
        return (block_of(m) < DEC_K) & (m >= EARLY)

    def with_y(m):
        return is_dec(m) | (m == LATE)

    def at(m):
        return pl.ds(pl.multiple_of(block_of(m) * CH, CH), CH)

    def pair_at(m):
        return rows(jnp.where(m < HALVED, lax.div(m, 2), m - HALVED // 2))

    def y_at(m):
        return rows(jnp.minimum(block_of(m), DEC_K) - EARLY)

    def core_copy(m, src):
        return far(src, out.at[:, at(m), :], core_s.at[m], core_r.at[m], {"tensor": mate})

    def corey_copy(m, src):
        return far(src, rcy.at[:, y_at(m), :], corey_s.at[m], corey_r.at[m], {"tensor": mate})

    def y_copy(m):
        cut = y_at(m)
        return far(
            yacc.at[:, cut, :], ry.at[:, cut, :], y_s.at[m], y_r.at[m], {"tensor": over}
        )

    def x_copy(m):
        return far(
            acc.at[1 - sec, at(m), :], rx.at[pair_at(m), :], x_s.at[m], x_r.at[m],
            {"section": 1 - sec},
        )

    def xc_copy(m):
        return far(
            acc.at[:, at(m), :], xc.at[:, pair_at(m), :], x_s.at[m], x_r.at[m],
            {"section": 1 - sec},
        )

    def z_copy(m, whole, right):
        if whole:
            src, dst = acc.at[:, at(m), :], (cl if right else cr).at[:, pair_at(m), :]
        else:
            src, dst = acc.at[sec, at(m), :], (zl if right else zr).at[pair_at(m), :]
        landed = zl_r if right else zr_r
        return far(src, dst, z_s.at[m], landed.at[m], {"dp": pos + 1 if right else pos - 1})

    def b_copy(m, whole, right):
        place = out.at[:, at(m), :] if whole else out.at[sec, at(m), :]
        sent = br_s if right else bl_s
        return far(place, place, sent.at[m], b_r.at[m], {"dp": pos + 1 if right else pos - 1})

    def a_copy(m):
        place = out.at[sec, at(m), :]
        return far(place, place, a_s.at[m], a_r.at[m], {"section": 1 - sec})

    def a_wait(m):
        place = out.at[1 - sec, at(m), :]
        far(place, place, a_s.at[m], a_r.at[m], {"section": 1 - sec}).wait_recv()

    give_enc().start()

    def start_core(m):
        @pl.when(is_dec(m))
        def _():
            core_copy(m, dec.at[mate, :, at(m), :]).start()
            corey_copy(m, dec.at[cross, :, at(m), :]).start()

    loop(MIXED, start_core)
    for load in loads:
        load.wait()

    def stage_c(m):
        @pl.when(m >= EARLY)
        def _():
            core_copy(m, out.at[:, at(m), :]).wait_recv()
            acc[:, at(m), :] = add(acc[:, at(m), :], out[:, at(m), :])

        @pl.when(with_y(m))
        def _():
            corey_copy(m, rcy.at[:, y_at(m), :]).wait_recv()
            yacc[:, y_at(m), :] = add(yacc[:, y_at(m), :], rcy[:, y_at(m), :])
            y_copy(m).start()

    def finished(m):
        @pl.when(block_of(m) == DEC_K - 1)
        def _():
            for step in range(1, LANES):
                emb_copy(step).start()
            emb[lane] = out[:, 512 : 512 + CH, :]

    def line_of(root, whole):
        left = pos < root
        right = pos > root
        here = pos == root
        reach = max(root, count - 1 - root)
        level = jnp.where(left, pos, jnp.where(right, count - 1 - pos, reach))
        dist = jnp.where(left, root - pos, pos - root)

        def view(ref, m):
            return ref.at[:, at(m), :] if whole else ref.at[sec, at(m), :]

        def landed(ref, m):
            return ref.at[:, pair_at(m), :] if whole else ref.at[pair_at(m), :]

        from_left, from_right = (cl, cr) if whole else (zl, zr)

        def outer(m):
            @pl.when(left & first)
            def _():
                z_copy(m, whole, True).start()

            @pl.when(right & last)
            def _():
                z_copy(m, whole, False).start()

        def inward(m):
            @pl.when(left & (pos > 0))
            def _():
                z_copy(m, whole, True).wait_recv()
                view(acc, m)[...] = add(view(acc, m)[...], landed(from_left, m)[...])
                z_copy(m, whole, True).start()

            @pl.when(right & (pos < count - 1))
            def _():
                z_copy(m, whole, False).wait_recv()
                view(acc, m)[...] = add(view(acc, m)[...], landed(from_right, m)[...])
                z_copy(m, whole, False).start()

            @pl.when(here)
            def _():
                total = view(acc, m)[...].astype(F32)
                if root > 0:
                    z_copy(m, whole, True).wait_recv()
                    total = total + landed(from_left, m)[...].astype(F32)
                if root < count - 1:
                    z_copy(m, whole, False).wait_recv()
                    total = total + landed(from_right, m)[...].astype(F32)
                if whole:
                    view(acc, m)[...] = total.astype(BF16)
                    xc_copy(m).start()
                else:
                    view(out, m)[...] = total.astype(BF16)
                    spread(m)
                    a_copy(m).start()

        def spread(m):
            if root > 0:
                b_copy(m, whole, False).start()
            if root < count - 1:
                b_copy(m, whole, True).start()

        def crossed(m):
            xc_copy(m).wait_recv()
            view(out, m)[...] = add(view(acc, m)[...], landed(xc, m)[...])
            spread(m)
            finished(m)

        def outward(m):
            b_copy(m, whole, False).wait_recv()

            @pl.when(left & (pos > 0))
            def _():
                b_copy(m, whole, False).start()

            @pl.when(right & (pos < count - 1))
            def _():
                b_copy(m, whole, True).start()

            if whole:
                finished(m)
            else:
                a_copy(m).start()

        def sent(m):
            @pl.when(jnp.logical_not(here))
            def _():
                z_copy(m, whole, True).wait_send()

            @pl.when((pos <= root) & (pos > 0))
            def _():
                b_copy(m, whole, False).wait_send()

            @pl.when((pos >= root) & (pos < count - 1))
            def _():
                b_copy(m, whole, True).wait_send()

            if whole:
                @pl.when(here)
                def _():
                    xc_copy(m).wait_send()
            else:
                x_copy(m).wait_send()
                a_copy(m).wait_send()

        def add_y(m):
            @pl.when(with_y(m))
            def _():
                y_copy(m).wait_recv()
                acc[:, at(m), :] = add(acc[:, at(m), :], ry[:, y_at(m), :])

            set_off(m)

        def set_off(m):
            if whole:
                outer(m)
            else:
                x_copy(m).start()

        def add_x(m):
            x_copy(m).wait_recv()
            acc[sec, at(m), :] = add(acc[sec, at(m), :], rx[pair_at(m), :])
            outer(m)

        def last_half(m):
            a_wait(m)
            finished(m)

        base = 1 if whole else 2
        back = base + reach + dist + (1 if whole else 0)
        steps = [(back, jnp.logical_not(here), outward), (base + level, level > 0, inward)]
        if whole:
            steps.append((base + reach + 1, here, crossed))
        else:
            steps += [(back + 1, True, last_half), (2, True, add_x)]
        return steps, sent, add_y, set_off

    low_root = (count - 1) // 2
    high_root = min(low_root + 1, count - 1)
    lines = [
        (lambda m: (lax.rem(m, 2) == 1) | (m >= HALVED), *line_of(low_root, False)),
        (lambda m: (lax.rem(m, 4) == 0) & (m < HALVED), *line_of(low_root, True)),
        (lambda m: (lax.rem(m, 4) == 2) & (m < HALVED), *line_of(high_root, True)),
    ]

    def finish(m):
        @pl.when(m >= EARLY)
        def _():
            core_copy(m, out.at[:, at(m), :]).wait_send()

        @pl.when(with_y(m))
        def _():
            corey_copy(m, rcy.at[:, y_at(m), :]).wait_send()
            y_copy(m).wait_send()

        for mine, _, sent, _, _ in lines:
            @pl.when(mine(m))
            def _(sent=sent):
                sent(m)

    far_reach = max(low_root, count - 1 - low_root, high_root, count - 1 - high_root)
    depth = LAG * (3 + 2 * far_reach) + 1

    def tick(n):
        @pl.when(n < LATE)
        def _():
            for low, high, piece in pieces:
                @pl.when((n >= low) & (n < high))
                def _(low=low, piece=piece):
                    piece(n - low)

        for mine, steps, _, add_y, _ in lines:
            m = n - LAG

            @pl.when((m >= EARLY) & (m < ALL_K) & mine(m))
            def _(m=m, add_y=add_y):
                add_y(m)

            for offset, enabled, stage in steps:
                m = n - LAG * offset

                @pl.when((m >= 0) & (m < ALL_K) & mine(m) & enabled)
                def _(m=m, stage=stage):
                    stage(m)

        @pl.when(n < ALL_K)
        def _():
            stage_c(n)

        @pl.when(n >= depth)
        def _():
            finish(n - depth)

    def set_off_early(m):
        for mine, _, _, _, set_off in lines:
            @pl.when(mine(m))
            def _(set_off=set_off):
                set_off(m)

    loop(EARLY, set_off_early)
    loop(ALL_K + depth, tick)

    for step in range(1, devices):
        dx_copy(step).wait()
    for step in range(1, LANES):
        emb_copy(step).wait()
    give_enc().wait_send()
    for k in range(D // 256):
        give_part(k, 0).wait_send()
        give_part(k, 1).wait_send()
        give_last(k).wait_send()


def backward_call(args, half, hid):
    dma = lambda *s: pltpu.SemaphoreType.DMA(s)
    vm = pltpu.VMEM
    full = ALL_K * CH
    y_half = DEC_ROWS - EARLY_ROWS + CH
    whole = HALVED // 2 * CH
    by_half = full - whole
    k = ALL_K
    rows = 2 * PAD
    cut = D // (2 * LANES)
    specs = [VM, VM] + [ANY] * 18 + [VM] * 3
    return pl.pallas_call(
        backward_and_sums,
        out_shape=[
            jax.ShapeDtypeStruct((2, full, D), BF16),
            jax.ShapeDtypeStruct((LANES, 2, CH, D), BF16),
            jax.ShapeDtypeStruct((2 * LANES, cut, VIS), BF16),
        ],
        in_specs=specs,
        out_specs=[VM] * 3,
        scratch_shapes=[
            vm((rows, D), BF16), vm((D, rows), BF16), vm((D, rows), BF16),
            vm((rows, D), F32), vm((rows, D), BF16), vm((rows, D), BF16),
            vm((2, rows, hid), BF16), vm((rows, D), BF16), vm((rows, D), F32),
            vm((rows, half), BF16), vm((2, 3, rows, half), BF16),
            vm((PAD, D), F32), vm((PAD, D), BF16), vm((PAD, D), BF16), vm((PAD, D), F32),
            vm((2 * LANES, cut, VIS), BF16),
            vm((2, 1, hid), F32), vm((2, 2, half), F32), vm((8, D), F32),
            vm((2, full, D), BF16), vm((2, y_half, D), BF16), vm((2, ENC_A + ENC_B, D), BF16),
            vm((2, y_half, D), BF16), vm((2, y_half, D), BF16),
            vm((by_half, D), BF16), vm((by_half, D), BF16), vm((by_half, D), BF16),
            vm((2, whole, D), BF16), vm((2, whole, D), BF16), vm((2, whole, D), BF16),
            vm((LANES, 32, D), F32), vm((LANES, 2, CH, D), BF16),
            *[vm(v.shape, v.dtype) for v in args[2:19]], dma(17), dma(2), dma(10), dma(10),
            dma(k), dma(k), dma(k), dma(k), dma(k), dma(k),
            dma(k), dma(k), dma(k), dma(k), dma(k),
            dma(k), dma(k), dma(k), dma(k), dma(k), dma(LANES), dma(LANES),
            dma(2 * LANES), dma(2 * LANES),
        ],
        compiler_params=pltpu.CompilerParams(
            collective_id=1, has_side_effects=True, vmem_limit_bytes=VMEM_LIMIT
        ),
    )(*args)


def finish_grads(
    total_h, emb_h, decoded, dx, *refs,
):
    (
        decoded_out, dx_out,
        e_qkv_h, e_qvb, e_proj_h, e_up_h, e_upb, e_down_h, e_gain, e_off,
        d_qkv_h, d_qvb, d_proj_h, d_up_h, d_upb, d_down_h, d_gain, d_off, d_ew_h, d_ev,
        total, emb, e_qkv, e_proj, e_up, e_down, d_qkv, d_proj, d_up, d_down, d_ew, in_s, out_s,
    ) = refs
    half = e_proj.shape[0]
    spots = ((A_TOP, B_TOP), (B_TOP, S_TOP + CH), (0, A_TOP))
    loads = [
        pltpu.make_async_copy(
            total_h.at[:, low:high, :], total.at[:, low:high, :], in_s.at[n]
        )
        for n, (low, high) in enumerate(spots)
    ] + [pltpu.make_async_copy(emb_h, emb, in_s.at[3])]
    for load in loads:
        load.start()
    stores = []

    def store(src, dst):
        copy = pltpu.make_async_copy(src, dst, out_s.at[len(stores)])
        copy.start()
        stores.append(copy)

    decoded_out[...] = decoded[...]
    dx_out[...] = dx[...]
    loads[0].wait()
    e_up[...] = total[0, A_TOP:B_TOP, :].astype(F32)
    store(e_up, e_up_h)
    e_down[...] = jnp.transpose(total[1, A_TOP:B_TOP, :].astype(F32))
    store(e_down, e_down_h)
    loads[1].wait()
    e_qkv[0] = total[0, B_TOP : B_TOP + half, :].astype(F32)
    e_qkv[1] = total[0, B_TOP + half : S_TOP, :].astype(F32)
    e_qkv[2] = total[1, B_TOP : B_TOP + half, :].astype(F32)
    store(e_qkv, e_qkv_h)
    e_proj[...] = total[1, B_TOP + half : S_TOP, :].astype(F32)
    store(e_proj, e_proj_h)
    loads[3].wait()
    for k in range(LANES):
        for h in range(2):
            top = k * 192 + h * 64
            d_ew[top : top + 64, :] = emb[k, h, :, 0:512].astype(F32)
            d_ew[k * 192 + 128 : (k + 1) * 192, h * 256 : (h + 1) * 256] = emb[
                k, h, :, 512:768
            ].astype(F32)
    store(d_ew, d_ew_h)
    loads[2].wait()

    def tile(number):
        h, top, col = tile_of(number)
        return total[h, top : top + CH, col : col + 256].astype(F32)

    for block in range(GRID // CH):
        rows = slice(block * CH, (block + 1) * CH)
        side = slice(block // 2 * 128, (block // 2 + 1) * 128)
        for k in range(2):
            d_up[rows, k * 256 : (k + 1) * 256] = tile(4 * block + k)
            if block % 2:
                both = jnp.concatenate([tile(4 * block - 2 + k), tile(4 * block + 2 + k)], 0)
                d_down[k * 256 : (k + 1) * 256, side] = jnp.transpose(both)
        one, two = tile(32 + 2 * block), tile(33 + 2 * block)
        d_qkv[0, rows, :] = one[:, 0:128]
        d_qkv[1, rows, :] = one[:, 128:256]
        d_qkv[2, rows, :] = two[:, 0:128]
        d_proj[block % 2 * CH : (block % 2 + 1) * CH, side] = two[:, 128:256]
    for src, dst in ((d_up, d_up_h), (d_down, d_down_h), (d_qkv, d_qkv_h), (d_proj, d_proj_h)):
        store(src, dst)
    little = total[0, S_TOP : S_TOP + 32, :].astype(F32)
    d_upb[...] = little[0, 0:512]
    d_qvb[0:1, :] = little[1:2, 0:128]
    d_qvb[1:2, :] = little[1:2, 128:256]
    e_upb[...] = little[2]
    e_qvb[0:1, :] = little[3:4, 0:192]
    e_qvb[1:2, :] = little[3:4, 256:448]
    d_gain[...] = little[8:10, 0:512]
    d_off[...] = little[10:14, 0:512]
    d_ev[...] = little[14:16, 0:512]
    e_gain[...] = little[16:18]
    e_off[...] = little[18:22]
    for copy in stores:
        copy.wait()


def finish_call(total, emb, decoded, dx, shapes):
    large = (0, 2, 3, 5, 8, 10, 11, 13, 16)
    order = (0, 2, 3, 5, 8, 10, 11, 13, 16)
    vm = pltpu.VMEM
    return pl.pallas_call(
        finish_grads,
        out_shape=[jax.ShapeDtypeStruct(v.shape, v.dtype) for v in (decoded, dx)]
        + [jax.ShapeDtypeStruct(s, F32) for s in shapes],
        in_specs=[ANY, ANY, VM, VM],
        out_specs=[VM, VM] + [ANY if n in large else VM for n in range(len(shapes))],
        scratch_shapes=[vm(total.shape, BF16), vm(emb.shape, BF16)]
        + [vm(shapes[n], F32) for n in order]
        + [pltpu.SemaphoreType.DMA((4,)), pltpu.SemaphoreType.DMA((9,))],
        compiler_params=pltpu.CompilerParams(vmem_limit_bytes=VMEM_LIMIT),
    )(total, emb, decoded, dx)


def position_rows():
    quarter = DD // 4
    freq = np.exp(np.arange(quarter, dtype=np.float32) * np.float32(-math.log(10000.0) / quarter))
    angle = np.arange(PAD, dtype=np.float32)[:, None] * freq[None, :].astype(np.float32)
    both = np.concatenate([np.sin(angle), np.cos(angle)], 1).astype(np.float32)
    high = both.astype(jnp.bfloat16)
    low = (both - high.astype(np.float32)).astype(jnp.bfloat16)
    return np.stack([high, low])


def per_device(
    patches, cotangent, widths, visible, window_shift, batch_order,
    encoder_qkv, encoder_qvbias, encoder_proj, encoder_up, encoder_upbias, encoder_down,
    encoder_gains, encoder_offsets,
    decoder_qkv, decoder_qvbias, decoder_proj, decoder_up, decoder_upbias, decoder_down,
    decoder_gains, decoder_offsets, embed_weight, embed_vectors,
):
    qkv0 = encoder_qkv.transpose(1, 2, 0)
    half = qkv0.shape[1]
    hid = encoder_up.shape[1]
    dff = decoder_up.shape[1] * LANES
    flat = patches.transpose(1, 0, 2).reshape(-1, D)
    (
        x, x1, a, u, y, gp, qkv, p, o, qkv1, proj1, up1, down1, dec_buf,
        d_enc, d_dqvb, d_dupb, d_dsmall, out_all,
    ) = forward_call(
        (
            widths, window_shift.T, batch_order, visible, flat, encoder_gains, encoder_offsets,
            encoder_qvbias, encoder_upbias, decoder_qvbias, decoder_upbias,
            qkv0, encoder_proj, encoder_up, encoder_down,
            decoder_qkv.transpose(1, 0, 2), decoder_proj, decoder_up, decoder_down,
            cotangent, embed_weight, embed_vectors, jnp.asarray(position_rows()),
            decoder_gains, decoder_offsets,
        ),
        half, hid, dff,
    )
    total, emb, dx_all = backward_call(
        (
            d_enc, encoder_gains, u, y, gp, encoder_down, down1, encoder_up, up1,
            x, x1, a, qkv, p, o, qkv0, qkv1, encoder_proj, proj1,
            dec_buf, d_dqvb, d_dupb, d_dsmall,
        ),
        half, hid,
    )
    out_all, dx_all, *grads = finish_call(
        total, emb, out_all, dx_all,
        [
            (3, half, D), (2, half), (half, D), (D, hid), (hid,), (hid, D), (2, D), (4, D),
            (3, DD, 128), (2, 128), (128, DD), (DD, 512), (512,), (512, DD), (2, DD), (4, DD),
            (D, DD), (2, DD),
        ],
    )
    grads[0] = grads[0].transpose(2, 0, 1)
    grads[8] = grads[8].transpose(1, 0, 2)
    return (out_all.swapaxes(1, 2), dx_all.swapaxes(1, 2), *grads)


def solution(mesh):
    weights = (
        P(None, None, "tensor"), P(None, "tensor"), P("tensor", None), P(None, "tensor"),
        P("tensor"), P("tensor", None), P(), P(),
    )
    split = P("dp", None, ("section", "tensor"))
    return jax.shard_map(
        per_device,
        mesh=mesh,
        in_specs=(
            P("dp", None, None), P("dp", None, None), P("dp"), P("dp", None), P("dp", None),
            P("dp", None),
        ) + weights + weights + (P(), P()),
        out_specs=(split, split) + weights + weights + (P(), P()),
        check_vma=False,
    )
```

profile of v0, /device:TPU:0, one launch (start us, length us, event | category | flops | bytes accessed | tf_op | source)
XLA Modules:
  0.0 222.6 jit_solution(16407720712742078353)
XLA Ops:
  0.7 79.7 %shard_map.392 = (f32[128,768]{1,0:T(8,128)}, f32[256,768]{1,0:T(8,128)}, bf16[256,768]{1,0:T(8,128)(2,1)}, bf16[256,768]{1,0:T(8,128)(2,1)}, bf16[2,256,768]{2,...) custom-call(s32[8]{0:T(128)} %wid.1, ...), custom_call_target="tpu_custom_call" | custom-call | tf_op jit(solution)/shard_map/pallas_call | solution.py:760
  80.4 133.5 %shard_map.393 = (bf16[2,1792,768]{2,1,0:T(8,128)(2,1)}, bf16[4,2,64,768]{3,2,1,0:T(8,128)(2,1)}, bf16[8,96,102]{2,1,0:T(8,128)(2,1)}) custom-call(bf16[128,768]{1,0:T(8,128)(2,1)} %get-tuple-element.62.d_enc, bf16[2,768]{1,0:T(2,128)(2,1)} %gains.3, bf16[256,768]{1,0:T(8,128)(2,1)} %get-tuple-element.63.h_u, bf16[2,256,768]{2,1,0:T(8,128)(2,1)} %get-tuple-element.64.h_y, ...), custom_call_target="tpu_custom_call" | custom-call | tf_op jit(solution)/shard_map/pallas_call | solution.py:1380
  213.9 8.6 %shard_map.394 = (bf16[8,64,512]{2,1,0:T(8,128)(2,1)}, bf16[8,96,102]{2,1,0:T(8,128)(2,1)}, f32[3,192,768]{2,1,0:T(8,128)}, f32[2,192]{1,0:T(2,128)}, f32[192,76...) custom-call(bf16[2,1792,768]{2,1,0:T(8,128)(2,1)} %get-tuple-element, ...), custom_call_target="tpu_custom_call" | custom-call | tf_op jit(solution)/shard_map/pallas_call | solution.py:1504
where the time goes:
time: 223 us
  Pallas kernels  222 us (100%)
    pallas_call x1, Pallas kernels, backward_call(): pl.pallas_call(backward_and_sums, out_shape=[jax.ShapeDtypeStruct((2, ful...  134 us
    pallas_call x1, Pallas kernels, forward_call(): pl.pallas_call(forward_and_decoder, out_shape=[jax.ShapeDtypeStruct(s, d)...  79.7 us
    pallas_call x1, Pallas kernels, finish_call(): pl.pallas_call(finish_grads, out_shape=[jax.ShapeDtypeStruct(v.shape, v.d...  8.56 us

commit v1 on v0

--- a/solution.py
+++ b/solution.py
@@ -163,9 +163,9 @@
 EARLY = 4
 EARLY_ROWS = EARLY * CH
 LAG = 2
-MIXED = EARLY + 2 * (DEC_K - EARLY)
-WAIT = 2
-LATE = 16
+ORDER = (0, 1, 2, 3, 4, 9, 10, 11, 12, 13, 14, 15, 16, 5, 17, 6, 7, 18, 19, 8, 21, 22, 23, 27, 20, 24, 25, 26)
+PIECES = (0, 0, 0, 2, 2, 4, 4, 5, 5, 11, 11, 13, 15, 15, 15, 17, 17, 17, 17, 17, 17, 19, 20)
+LATE = ORDER.index(B_K)
 HALVED = ALL_K - 4
 
 
@@ -491,14 +491,9 @@
     def dec_bias(row, size):
         return jnp.concatenate([biases[k, row : row + 1, 0:size] for k in range(LANES)], 1)
 
-    def project(i):
-        r = span(i, 256)
-        rows = a[r, :]
-        acts[0, r, :] = (nn(rows, qkv[0]) + dec_bias(4, 128)).astype(BF16)
-        acts[1, r, :] = nn(rows, qkv[1]).astype(BF16)
-        acts[2, r, :] = (nn(rows, qkv[2]) + dec_bias(5, 128)).astype(BF16)
-
-    loop(2, project)
+    acts[0] = (nn(a[...], qkv[0]) + dec_bias(4, 128)).astype(BF16)
+    acts[1] = nn(a[...], qkv[1]).astype(BF16)
+    acts[2] = (nn(a[...], qkv[2]) + dec_bias(5, 128)).astype(BF16)
     pass_on(1)
     pass_on(2)
     marks = head_marks(128, DEC_SIZE, BF16)
@@ -529,7 +524,7 @@
     arrived(1)
 
     def mix(i):
-        r = span(i, PAD)
+        r = span(i, 256)
         x = x0[r, :] + nn(o[r, :], proj[...]) + offsets[2:3]
         x1[r, :] = x
         hat, _ = normal(x)
@@ -537,28 +532,24 @@
         u[r, :] = un.astype(BF16)
         ut[:, r] = jnp.transpose(un).astype(BF16)
 
-    loop(GRID // PAD, mix, unroll=2)
+    loop(2, mix)
     pass_last(3)
     arrived(2)
 
     def ff(i):
-        k = lax.div(i, 4)
-        side = lax.rem(lax.div(i, 2), 2)
-        c = span(lax.div(i, 2), 256)
-        r = span(lax.rem(i, 2), 256)
-        h = nn(u[r, :], up[:, c]) + biases[k, 3:4, span(side, 256)]
+        c = span(i, 256)
+        h = nn(u[...], up[:, c]) + biases[lax.div(i, 2), 3:4, span(lax.rem(i, 2), 256)]
         act, slope = gelu_both(h)
-        y[r, c] = act.astype(BF16)
-        gp[r, c] = slope.astype(BF16)
-
-    loop(2 * up.shape[1] // 256, ff, unroll=2)
+        y[:, c] = act.astype(BF16)
+        gp[:, c] = slope.astype(BF16)
+
+    loop(up.shape[1] // 256, ff, unroll=2)
     arrived(3)
     def out(i):
-        r = span(lax.rem(i, 2), 256)
-        c = span(lax.div(i, 2), 256)
-        acc[r, c] = nn(y[r, :], down[:, c])
-
-    loop(4, out, unroll=2)
+        c = span(i, 256)
+        acc[:, c] = nn(y[...], down[:, c])
+
+    loop(2, out)
     full = ((acc[...] + x1[...] + offsets[3:4]) * valid_rows()).astype(BF16)
     turned = tn(full, perm[...]).astype(BF16)
     for k in range(devices):
@@ -623,14 +614,13 @@
     loop(LANES, ff_step)
 
     def ff_in(i):
-        r = span(lax.rem(i, 2), 256)
-        c = span(lax.div(i, 2), 256)
-        acc[r, c] = nt(gp[r, :], up[c, :])
-
-    loop(4, ff_in, unroll=2)
+        c = span(i, 256)
+        acc[:, c] = nt(gp[...], up[c, :])
+
+    loop(2, ff_in)
 
     def mix_back(i):
-        r = span(i, PAD)
+        r = span(i, 256)
         hat, scale = normal(x1[r, :])
         da = acc[r, :]
         dx = g32[r, :] + normal_back(da, hat, scale, gain[1:2])
@@ -642,7 +632,7 @@
         gb[r, :] = dxb
         u[r, :] = nt(dxb, proj[...]).astype(BF16)
 
-    loop(GRID // PAD, mix_back, unroll=2)
+    loop(2, mix_back)
     early_core(0).wait_recv()
     early_add(lane, e_rc)
     d_proj = tn(o[...], gb[...]).astype(BF16)
@@ -668,15 +658,12 @@
     d_qvb[1:2, :] = colsum(acts[2].astype(F32))
 
     def project_back(i):
-        r = span(lax.rem(i, 2), 256)
-        c = span(lax.div(i, 2), 256)
-        acc[r, c] = (
-            nt(acts[0, r, :], qkv[0, c, :])
-            + nt(acts[1, r, :], qkv[1, c, :])
-            + nt(acts[2, r, :], qkv[2, c, :])
+        c = span(i, 256)
+        acc[:, c] = (
+            nt(acts[0], qkv[0, c, :]) + nt(acts[1], qkv[1, c, :]) + nt(acts[2], qkv[2, c, :])
         )
 
-    loop(4, project_back, unroll=2)
+    loop(2, project_back)
     gt[...] = jnp.transpose(a[...].astype(F32)).astype(BF16)
     for j in range(3):
         d_qkv = nn(gt[...], acts[j]).astype(BF16)
@@ -910,8 +897,7 @@
         give_part(i, 0).start()
         give_part(i, 1).start()
 
-    def norm_two(i):
-        del i
+    def norm_two():
         for fetch in fetches[7:]:
             fetch.wait()
         for k in range(D // 256):
@@ -936,24 +922,22 @@
 
         loop(2 * PAD // 64, body)
 
-    def attention(g, proj):
-        d_proj = tn(o[g], gx[...]).astype(BF16)
-        if g == 0:
-            acc[1, B_TOP + width : S_TOP, :] = d_proj
-        else:
-            enc_mate[1, ENC_A + width : ENC_A + 2 * width, :] = d_proj
-        d_o[...] = nt(gx[...], proj[...]).astype(BF16)
-        for c in range(2):
-            r = slice(c * PAD, (c + 1) * PAD)
-            dq, dk, dv = attend_back(
-                qkv[g, 0, r], qkv[g, 1, r], qkv[g, 2, r], p[g, c], o[g, r], 1.0 / nn(p[g, c], ones),
-                d_o[r, :], marks, marks32, None, ones, ENC_SCALE,
-            )
-            d_acts[g, 0, r] = dq
-            d_acts[g, 1, r] = dk
-            d_acts[g, 2, r] = dv
-        d_qvb[g, 0:1, :] = colsum(d_acts[g, 0].astype(F32))
-        d_qvb[g, 1:2, :] = colsum(d_acts[g, 2].astype(F32))
+    def attention(g, c):
+        if c == 0:
+            d_proj = tn(o[g], gx[...]).astype(BF16)
+            if g == 0:
+                acc[1, B_TOP + width : S_TOP, :] = d_proj
+            else:
+                enc_mate[1, ENC_A + width : ENC_A + 2 * width, :] = d_proj
+            d_o[...] = nt(gx[...], (proj0, proj1)[g][...]).astype(BF16)
+        r = slice(c * PAD, (c + 1) * PAD)
+        d_acts[g, 0, r], d_acts[g, 1, r], d_acts[g, 2, r] = attend_back(
+            qkv[g, 0, r], qkv[g, 1, r], qkv[g, 2, r], p[g, c], o[g, r], 1.0 / nn(p[g, c], ones),
+            d_o[r, :], marks, marks32, None, ones, ENC_SCALE,
+        )
+        if c == 1:
+            d_qvb[g, 0:1, :] = colsum(d_acts[g, 0].astype(F32))
+            d_qvb[g, 1:2, :] = colsum(d_acts[g, 2].astype(F32))
 
     def project_in(i):
         c = rows(i, 256)
@@ -974,8 +958,7 @@
             else:
                 enc_mate[j // 2, ENC_A + row : ENC_A + row + width, :] = d
 
-    def norm_one(i):
-        del i
+    def norm_one():
         for k in range(D // 256):
             give_last(k).wait_recv()
 
@@ -1023,29 +1006,42 @@
 
         loop(ALL_K, body)
 
-    def first_piece(i):
-        del i
+    def first_piece():
         for fetch in fetches[:7]:
             fetch.wait()
         ut[...] = jnp.transpose(u[...].astype(F32)).astype(BF16)
         give_enc().wait_recv()
         gt[...] = jnp.transpose(gb[...].astype(F32)).astype(BF16)
 
-    pieces = [(WAIT, WAIT + 1, first_piece)]
-    for g, down in enumerate((down0, down1)):
-        pieces.append((WAIT, WAIT + 3, lambda i, g=g, down=down: ff_back(g, i, down)))
-    pieces.append((WAIT + 3, WAIT + 4, lambda i: core_enc(DEC_K, DEC_K + ENC_A // CH)))
-    pieces.append((WAIT + 3, WAIT + 4, lambda i: loop(D // 256, ff_in)))
-    pieces.append((WAIT + 6, WAIT + 7, norm_two))
-    for g, proj in enumerate((proj0, proj1)):
-        low = WAIT + 7 + g
-        pieces.append((low, low + 1, lambda i, g=g, proj=proj: attention(g, proj)))
-    pieces.append((WAIT + 9, WAIT + 10, lambda i: loop(D // 256, project_in)))
-    for g in range(2):
-        low = WAIT + 10 + g
-        pieces.append((low, low + 1, lambda i, g=g: project_grad(g)))
-    pieces.append((WAIT + 12, WAIT + 13, lambda i: core_enc(DEC_K + ENC_A // CH, B_K)))
-    pieces.append((WAIT + 13, WAIT + 14, norm_one))
+    def ff_step(k):
+        for g, down in enumerate((down0, down1)):
+            @pl.when(lax.rem(k, 2) == g)
+            def _(g=g, down=down):
+                ff_back(g, lax.div(k, 2), down)
+
+    def run_pieces(n):
+        def several(low, high, body):
+            begin = sum(jnp.where(n > t, 1, 0) for t in PIECES[low:high])
+            end = sum(jnp.where(n >= t, 1, 0) for t in PIECES[low:high])
+            lax.fori_loop(begin, end, lambda k, c: (body(k), c)[1], 0)
+
+        def single(k, body):
+            @pl.when(n == PIECES[k])
+            def _():
+                body()
+
+        single(0, first_piece)
+        several(1, 7, ff_step)
+        single(7, lambda: core_enc(DEC_K, DEC_K + ENC_A // CH))
+        several(8, 11, ff_in)
+        single(11, norm_two)
+        for k in range(4):
+            single(12 + k, lambda k=k: attention(k // 2, k % 2))
+        several(16, 19, project_in)
+        for g in range(2):
+            single(19 + g, lambda g=g: project_grad(g))
+        single(21, lambda: core_enc(DEC_K + ENC_A // CH, B_K))
+        single(22, norm_one)
 
     def dx_copy(step):
         peer, place = group_peer(step)
@@ -1058,10 +1054,11 @@
         )
 
     def block_of(m):
-        even = lax.rem(m - EARLY, 2) == 0
-        turn = jnp.where(even, EARLY + lax.div(m - EARLY, 2), DEC_K + lax.div(m - EARLY - 1, 2))
-        late = jnp.where(m == LATE, ALL_K - 1, jnp.where(m > LATE, m - 1, m))
-        return jnp.where(m < EARLY, m, jnp.where(m >= MIXED, late, turn))
+        shift = 0
+        for k in range(1, ALL_K):
+            if ORDER[k] - k != ORDER[k - 1] - k + 1:
+                shift = jnp.where(m >= k, ORDER[k] - k, shift)
+        return m + shift
 
     def is_dec(m):
         return (block_of(m) < DEC_K) & (m >= EARLY)
@@ -1072,7 +1069,7 @@
     def at(m):
         return pl.ds(pl.multiple_of(block_of(m) * CH, CH), CH)
 
-    def pair_at(m):
+    def slot_at(m):
         return rows(jnp.where(m < HALVED, lax.div(m, 2), m - HALVED // 2))
 
     def y_at(m):
@@ -1092,21 +1089,21 @@
 
     def x_copy(m):
         return far(
-            acc.at[1 - sec, at(m), :], rx.at[pair_at(m), :], x_s.at[m], x_r.at[m],
+            acc.at[1 - sec, at(m), :], rx.at[slot_at(m), :], x_s.at[m], x_r.at[m],
             {"section": 1 - sec},
         )
 
     def xc_copy(m):
         return far(
-            acc.at[:, at(m), :], xc.at[:, pair_at(m), :], x_s.at[m], x_r.at[m],
+            acc.at[:, at(m), :], xc.at[:, slot_at(m), :], x_s.at[m], x_r.at[m],
             {"section": 1 - sec},
         )
 
     def z_copy(m, whole, right):
         if whole:
-            src, dst = acc.at[:, at(m), :], (cl if right else cr).at[:, pair_at(m), :]
+            src, dst = acc.at[:, at(m), :], (cl if right else cr).at[:, slot_at(m), :]
         else:
-            src, dst = acc.at[sec, at(m), :], (zl if right else zr).at[pair_at(m), :]
+            src, dst = acc.at[sec, at(m), :], (zl if right else zr).at[slot_at(m), :]
         landed = zl_r if right else zr_r
         return far(src, dst, z_s.at[m], landed.at[m], {"dp": pos + 1 if right else pos - 1})
 
@@ -1131,7 +1128,7 @@
             core_copy(m, dec.at[mate, :, at(m), :]).start()
             corey_copy(m, dec.at[cross, :, at(m), :]).start()
 
-    loop(MIXED, start_core)
+    loop(ALL_K, start_core)
     for load in loads:
         load.wait()
 
@@ -1166,7 +1163,7 @@
             return ref.at[:, at(m), :] if whole else ref.at[sec, at(m), :]
 
         def landed(ref, m):
-            return ref.at[:, pair_at(m), :] if whole else ref.at[pair_at(m), :]
+            return ref.at[:, slot_at(m), :] if whole else ref.at[slot_at(m), :]
 
         from_left, from_right = (cl, cr) if whole else (zl, zr)
 
@@ -1274,7 +1271,7 @@
 
         def add_x(m):
             x_copy(m).wait_recv()
-            acc[sec, at(m), :] = add(acc[sec, at(m), :], rx[pair_at(m), :])
+            acc[sec, at(m), :] = add(acc[sec, at(m), :], rx[slot_at(m), :])
             outer(m)
 
         def last_half(m):
@@ -1317,26 +1314,27 @@
     depth = LAG * (3 + 2 * far_reach) + 1
 
     def tick(n):
-        @pl.when(n < LATE)
+        @pl.when(n <= PIECES[-1])
         def _():
-            for low, high, piece in pieces:
-                @pl.when((n >= low) & (n < high))
-                def _(low=low, piece=piece):
-                    piece(n - low)
+            run_pieces(n)
 
         for mine, steps, _, add_y, _ in lines:
             m = n - LAG
 
-            @pl.when((m >= EARLY) & (m < ALL_K) & mine(m))
-            def _(m=m, add_y=add_y):
-                add_y(m)
+            @pl.when((m >= EARLY) & (m < ALL_K))
+            def _(m=m, mine=mine, add_y=add_y):
+                @pl.when(mine(m))
+                def _():
+                    add_y(m)
 
             for offset, enabled, stage in steps:
                 m = n - LAG * offset
 
-                @pl.when((m >= 0) & (m < ALL_K) & mine(m) & enabled)
-                def _(m=m, stage=stage):
-                    stage(m)
+                @pl.when((m >= 0) & (m < ALL_K) & enabled)
+                def _(m=m, mine=mine, stage=stage):
+                    @pl.when(mine(m))
+                    def _():
+                        stage(m)
 
         @pl.when(n < ALL_K)
         def _():
@@ -1399,7 +1397,8 @@
             vm((by_half, D), BF16), vm((by_half, D), BF16), vm((by_half, D), BF16),
             vm((2, whole, D), BF16), vm((2, whole, D), BF16), vm((2, whole, D), BF16),
             vm((LANES, 32, D), F32), vm((LANES, 2, CH, D), BF16),
-            *[vm(v.shape, v.dtype) for v in args[2:19]], dma(17), dma(2), dma(10), dma(10),
+            *[vm(v.shape, v.dtype) for v in args[2:19]],
+            dma(17), dma(2), dma(10), dma(10),
             dma(k), dma(k), dma(k), dma(k), dma(k), dma(k),
             dma(k), dma(k), dma(k), dma(k), dma(k),
             dma(k), dma(k), dma(k), dma(k), dma(k), dma(LANES), dma(LANES),
@@ -1412,55 +1411,19 @@
 
 
 def finish_grads(
-    total_h, emb_h, decoded, dx, *refs,
+    total, emb, decoded, dx, decoded_out, dx_out,
+    e_qkv, e_qvb, e_proj, e_up, e_upb, e_down, e_gain, e_off,
+    d_qkv, d_qvb, d_proj, d_up, d_upb, d_down, d_gain, d_off, d_ew, d_ev,
 ):
-    (
-        decoded_out, dx_out,
-        e_qkv_h, e_qvb, e_proj_h, e_up_h, e_upb, e_down_h, e_gain, e_off,
-        d_qkv_h, d_qvb, d_proj_h, d_up_h, d_upb, d_down_h, d_gain, d_off, d_ew_h, d_ev,
-        total, emb, e_qkv, e_proj, e_up, e_down, d_qkv, d_proj, d_up, d_down, d_ew, in_s, out_s,
-    ) = refs
     half = e_proj.shape[0]
-    spots = ((A_TOP, B_TOP), (B_TOP, S_TOP + CH), (0, A_TOP))
-    loads = [
-        pltpu.make_async_copy(
-            total_h.at[:, low:high, :], total.at[:, low:high, :], in_s.at[n]
-        )
-        for n, (low, high) in enumerate(spots)
-    ] + [pltpu.make_async_copy(emb_h, emb, in_s.at[3])]
-    for load in loads:
-        load.start()
-    stores = []
-
-    def store(src, dst):
-        copy = pltpu.make_async_copy(src, dst, out_s.at[len(stores)])
-        copy.start()
-        stores.append(copy)
-
     decoded_out[...] = decoded[...]
     dx_out[...] = dx[...]
-    loads[0].wait()
     e_up[...] = total[0, A_TOP:B_TOP, :].astype(F32)
-    store(e_up, e_up_h)
     e_down[...] = jnp.transpose(total[1, A_TOP:B_TOP, :].astype(F32))
-    store(e_down, e_down_h)
-    loads[1].wait()
     e_qkv[0] = total[0, B_TOP : B_TOP + half, :].astype(F32)
     e_qkv[1] = total[0, B_TOP + half : S_TOP, :].astype(F32)
     e_qkv[2] = total[1, B_TOP : B_TOP + half, :].astype(F32)
-    store(e_qkv, e_qkv_h)
     e_proj[...] = total[1, B_TOP + half : S_TOP, :].astype(F32)
-    store(e_proj, e_proj_h)
-    loads[3].wait()
-    for k in range(LANES):
-        for h in range(2):
-            top = k * 192 + h * 64
-            d_ew[top : top + 64, :] = emb[k, h, :, 0:512].astype(F32)
-            d_ew[k * 192 + 128 : (k + 1) * 192, h * 256 : (h + 1) * 256] = emb[
-                k, h, :, 512:768
-            ].astype(F32)
-    store(d_ew, d_ew_h)
-    loads[2].wait()
 
     def tile(number):
         h, top, col = tile_of(number)
@@ -1479,8 +1442,13 @@
         d_qkv[1, rows, :] = one[:, 128:256]
         d_qkv[2, rows, :] = two[:, 0:128]
         d_proj[block % 2 * CH : (block % 2 + 1) * CH, side] = two[:, 128:256]
-    for src, dst in ((d_up, d_up_h), (d_down, d_down_h), (d_qkv, d_qkv_h), (d_proj, d_proj_h)):
-        store(src, dst)
+    for k in range(LANES):
+        for h in range(2):
+            top = k * 192 + h * 64
+            d_ew[top : top + 64, :] = emb[k, h, :, 0:512].astype(F32)
+            d_ew[k * 192 + 128 : (k + 1) * 192, h * 256 : (h + 1) * 256] = emb[
+                k, h, :, 512:768
+            ].astype(F32)
     little = total[0, S_TOP : S_TOP + 32, :].astype(F32)
     d_upb[...] = little[0, 0:512]
     d_qvb[0:1, :] = little[1:2, 0:128]
@@ -1493,25 +1461,17 @@
     d_ev[...] = little[14:16, 0:512]
     e_gain[...] = little[16:18]
     e_off[...] = little[18:22]
-    for copy in stores:
-        copy.wait()
-
-
-def finish_call(total, emb, decoded, dx, shapes):
-    large = (0, 2, 3, 5, 8, 10, 11, 13, 16)
-    order = (0, 2, 3, 5, 8, 10, 11, 13, 16)
-    vm = pltpu.VMEM
+
+
+def call(kernel, specs, shapes, scratch, args):
     return pl.pallas_call(
-        finish_grads,
-        out_shape=[jax.ShapeDtypeStruct(v.shape, v.dtype) for v in (decoded, dx)]
-        + [jax.ShapeDtypeStruct(s, F32) for s in shapes],
-        in_specs=[ANY, ANY, VM, VM],
-        out_specs=[VM, VM] + [ANY if n in large else VM for n in range(len(shapes))],
-        scratch_shapes=[vm(total.shape, BF16), vm(emb.shape, BF16)]
-        + [vm(shapes[n], F32) for n in order]
-        + [pltpu.SemaphoreType.DMA((4,)), pltpu.SemaphoreType.DMA((9,))],
+        kernel,
+        out_shape=[jax.ShapeDtypeStruct(s, d) for s, d in shapes],
+        in_specs=specs,
+        out_specs=[VM] * len(shapes),
+        scratch_shapes=scratch,
         compiler_params=pltpu.CompilerParams(vmem_limit_bytes=VMEM_LIMIT),
-    )(total, emb, decoded, dx)
+    )(*args)
 
 
 def position_rows():
@@ -1558,13 +1518,15 @@
         ),
         half, hid,
     )
-    out_all, dx_all, *grads = finish_call(
-        total, emb, out_all, dx_all,
+    f = lambda *shape: (shape, F32)
+    out_all, dx_all, *grads = call(
+        finish_grads, [VM] * 4,
         [
-            (3, half, D), (2, half), (half, D), (D, hid), (hid,), (hid, D), (2, D), (4, D),
-            (3, DD, 128), (2, 128), (128, DD), (DD, 512), (512,), (512, DD), (2, DD), (4, DD),
-            (D, DD), (2, DD),
+            (out_all.shape, BF16), (dx_all.shape, BF16), f(3, half, D), f(2, half), f(half, D), f(D, hid), f(hid), f(hid, D), f(2, D), f(4, D),
+            f(3, DD, 128), f(2, 128), f(128, DD), f(DD, 512), f(512), f(512, DD), f(2, DD), f(4, DD),
+            f(D, DD), f(2, DD),
         ],
+        [], (total, emb, out_all, dx_all),
     )
     grads[0] = grads[0].transpose(2, 0, 1)
     grads[8] = grads[8].transpose(1, 0, 2)

time: 223 us -> 219 us (0.982)
  Pallas kernels: 222 us -> 218 us
    pallas_call x1, Pallas kernels: 134 us -> 131 us  [backward_call(): pl.pallas_call(backward_and_sums, out_shape=[jax.ShapeDtypeStruct((2, ful...]
where the time goes in v1:
time: 219 us
  Pallas kernels  218 us (100%)
    pallas_call x1, Pallas kernels, backward_call(): pl.pallas_call(backward_and_sums, out_shape=[jax.ShapeDtypeStruct((2, ful...  131 us
    pallas_call x1, Pallas kernels, forward_call(): pl.pallas_call(forward_and_decoder, out_shape=[jax.ShapeDtypeStruct(s, d)...  79 us
    pallas_call x1, Pallas kernels, call(): pl.pallas_call(kernel, out_shape=[jax.ShapeDtypeStruct(s, d) for s, d in...  8.08 us

profile of v1, /device:TPU:0, one launch (start us, length us, event | category | flops | bytes accessed | tf_op | source)
XLA Modules:
  0.0 218.6 jit_solution(927259149247237004)
XLA Ops:
  0.7 79.0 %shard_map.392 = (f32[128,768]{1,0:T(8,128)}, f32[256,768]{1,0:T(8,128)}, bf16[256,768]{1,0:T(8,128)(2,1)}, bf16[256,768]{1,0:T(8,128)(2,1)}, bf16[2,256,768]{2,...) custom-call(s32[8]{0:T(128)} %wid.1, ...), custom_call_target="tpu_custom_call" | custom-call | tf_op jit(solution)/shard_map/pallas_call | solution.py:747
  79.6 130.8 %shard_map.393 = (bf16[2,1792,768]{2,1,0:T(8,128)(2,1)}, bf16[4,2,64,768]{3,2,1,0:T(8,128)(2,1)}, bf16[8,96,102]{2,1,0:T(8,128)(2,1)}) custom-call(bf16[128,768]{1,0:T(8,128)(2,1)} %get-tuple-element.62.d_enc, bf16[2,768]{1,0:T(2,128)(2,1)} %gains.3, bf16[256,768]{1,0:T(8,128)(2,1)} %get-tuple-element.63.h_u, bf16[2,256,768]{2,1,0:T(8,128)(2,1)} %get-tuple-element.64.h_y, ...), custom_call_target="tpu_custom_call" | custom-call | tf_op jit(solution)/shard_map/pallas_call | solution.py:1378
  210.5 8.1 %shard_map.394 = (bf16[8,64,512]{2,1,0:T(8,128)(2,1)}, bf16[8,96,102]{2,1,0:T(8,128)(2,1)}, f32[3,192,768]{2,1,0:T(8,128)}, f32[2,192]{1,0:T(2,128)}, f32[192,76...) custom-call(bf16[2,1792,768]{2,1,0:T(8,128)(2,1)} %get-tuple-element, ...), custom_call_target="tpu_custom_call" | custom-call | tf_op jit(solution)/shard_map/pallas_call | solution.py:1467
